TPU v7x, 32 devices: a whole 2x2x4 slice. The times are simulated.
32 devices in a mesh: dp: 4 (over x, core), heads: 8 (over z, y).
Axes of the slice: x: 2, y: 2, z: 4, core: 2. Of those that a mesh axis runs over, the one named last changes fastest.
Arguments:
- latent: bfloat16 [4, 512, 512], P(None, 'dp'), may hold values from -6 to 6
- rope_keys: bfloat16 [4, 512, 64], P(None, 'dp'), may hold values from -6 to 6
- queries: bfloat16 [4, 512, 24576], P(None, 'dp', 'heads'), may hold values from -320 to 320
- grad_out: bfloat16 [4, 512, 16384], P(None, 'dp', 'heads'), may hold values from -2 to 2
- key_value_up_weight: bfloat16 [4, 512, 32768], P('dp', None, 'heads'), may hold values from -0.25 to 0.25
- momentum: bfloat16 [4, 512, 32768], P('dp', None, 'heads'), may hold values from -16 to 16
Outputs:
- new_momentum: bfloat16 [4, 512, 32768], P('dp', None, 'heads')
- layer_update_step: float32 [4, 512, 32768], P('dp', None, 'heads')
All inputs are finite; a program needn't handle non-finite values.
Results may differ from a plain program's by a relative error of at most 0.015.
Values may be sent and summed in bfloat16 or wider, within the bound.
A program may use at most 128 MiB of HBM per device.

v0:
```python
import math

import jax
import jax.numpy as jnp
from jax import lax
from jax.sharding import PartitionSpec as P

LATENT = 512
HEADS = 128
NOPE = 128
ROPE = 64
VDIM = 128
STEPS = 2


poly_first = 3.4445
poly_second = -4.775
poly_third = 2.0315
norm_epsilon = 1e-07
decay_rate = 0.95


def layer_grads(compressed_latent_rows, rotary_position_rows, query_rows, grad_rows, weight_cols):
    rows = compressed_latent_rows.shape[0]
    heads_here = query_rows.shape[1] // (NOPE + ROPE)
    score_scale = 1.0 / math.sqrt(NOPE + ROPE)
    kv_rows = jnp.dot(
        compressed_latent_rows, weight_cols, preferred_element_type=jnp.float32
    ).astype(jnp.bfloat16)
    kv_rows = kv_rows.reshape(rows, heads_here, NOPE + VDIM)
    key_nope = kv_rows[:, :, :NOPE]
    values = kv_rows[:, :, NOPE:]
    query_all = query_rows.reshape(rows, heads_here, NOPE + ROPE)
    query_nope = query_all[:, :, :NOPE]
    query_rope = query_all[:, :, NOPE:]
    scores = jnp.einsum("shd,thd->hst", query_nope, key_nope, preferred_element_type=jnp.float32)
    scores = scores + jnp.einsum(
        "shd,td->hst", query_rope, rotary_position_rows, preferred_element_type=jnp.float32
    )
    scores = scores * score_scale
    places = jnp.arange(rows)
    allowed = places[None, :] <= places[:, None]
    scores = jnp.where(allowed[None], scores, -jnp.inf)
    top_score = jnp.max(scores, axis=-1, keepdims=True)
    expd = jnp.exp(scores - top_score)
    probs = expd / jnp.sum(expd, axis=-1, keepdims=True)
    probs_low = probs.astype(jnp.bfloat16)
    grad_heads = grad_rows.reshape(rows, heads_here, VDIM)
    grad_values = jnp.einsum(
        "hst,shd->thd", probs_low, grad_heads, preferred_element_type=jnp.float32
    )
    grad_probs = jnp.einsum("shd,thd->hst", grad_heads, values, preferred_element_type=jnp.float32)
    row_delta = jnp.sum(probs * grad_probs, axis=-1, keepdims=True)
    grad_scores = (probs * (grad_probs - row_delta) * score_scale).astype(jnp.bfloat16)
    grad_keys = jnp.einsum(
        "hst,shd->thd", grad_scores, query_nope, preferred_element_type=jnp.float32
    )
    joined = jnp.concatenate([grad_keys, grad_values], axis=-1).astype(jnp.bfloat16)
    return joined.reshape(rows, heads_here * (NOPE + VDIM))


def body(latent, rope_keys, queries, grad_out, key_value_up_weight, momentum):
    highest = lax.Precision.HIGHEST
    weights_all = lax.all_gather(key_value_up_weight, "dp", axis=0, tiled=True)

    def layer_body(carry, inputs):
        return (carry, layer_grads(inputs[0], inputs[1], inputs[2], inputs[3], inputs[4]))

    unused, key_value_gradient_total = lax.scan(
        layer_body, 0, (latent, rope_keys, queries, grad_out, weights_all)
    )
    grads = lax.psum_scatter(
        jnp.einsum(
            "eot,eov->etv", latent, key_value_gradient_total, preferred_element_type=jnp.float32
        ).astype(jnp.bfloat16),
        "dp",
        scatter_dimension=0,
        tiled=True,
    ).astype(jnp.float32)
    fresh = (decay_rate * momentum.astype(jnp.float32) + grads).astype(jnp.bfloat16)
    source = fresh[0].astype(jnp.float32)
    gram_raw = lax.psum(
        jnp.dot(source, source.T, precision=highest).astype(jnp.bfloat16), "heads"
    ).astype(jnp.float32)
    norm_value = jnp.sqrt(jnp.trace(gram_raw)) + norm_epsilon
    base = gram_raw / (norm_value * norm_value)
    identity_matrix = jnp.eye(source.shape[0], dtype=jnp.float32)
    mixer = identity_matrix
    for count_index in range(STEPS):
        inner = jnp.dot(jnp.dot(mixer, base, precision=highest), mixer.T, precision=highest)
        poly = (
            poly_first * identity_matrix
            + poly_second * inner
            + poly_third * jnp.dot(inner, inner, precision=highest)
        )
        mixer = jnp.dot(poly, mixer, precision=highest)
    iterate = jnp.dot(mixer, source, precision=highest) / norm_value
    update_scale = 0.2 * math.sqrt(max(LATENT, HEADS * (NOPE + VDIM)))
    return (fresh, (update_scale * iterate)[None])


def solution(mesh):
    placed = (
        P(None, "dp", None),
        P(None, "dp", None),
        P(None, "dp", "heads"),
        P(None, "dp", "heads"),
        P("dp", None, "heads"),
        P("dp", None, "heads"),
    )
    return jax.shard_map(
        body,
        mesh=mesh,
        in_specs=placed,
        out_specs=(P("dp", None, "heads"), P("dp", None, "heads")),
        check_vma=False,
    )
```

profile of v0, /device:TPU:24, one launch (start us, length us, event | category | flops | bytes accessed | tf_op | source)
XLA Modules:
  0.0 424.6 jit_solution(3763998489545131249)
XLA Ops:
  8.0 108.5 %all-gather.2.cloned.1.call-done = bf16[4,512,4096]{2,1,0:T(8,128)(2,1)} async-done(((bf16[1,512,4096]{2,1,0:T(8,128)(2,1)}), bf16[4,512,4096]{2,1,0:T(8,128)(2,1)}) %all-gather.2.cloned.1.call-update) | async-done | bytes 16777232 | tf_op jit(solution)/shard_map/all_gather | solution.py:64
  116.5 58.0 %while.10 = (s32[]{:T(128)}, bf16[4,128,4096]{1,2,0:T(8,128)(2,1)}, bf16[4,128,3072]{2,1,0:T(8,128)(2,1)}, bf16[4,128,512]{2,1,0:T(8,128)(2,1)S(1)}, bf16[4,512,...) while((s32[]{:T(128)}, bf16[4,128,4096]{1,2,0:T(8,128)(2,1)}, ...), condition=%wide.region_4.5_spmd, body=%wide.region_0.4_spmd.sunk | while | flops 845959552 | bytes 37177472 | solution.py:69
  116.5 1.2 constant_dynamic-slice_fusion.5
  119.1 2.9 convolution_convert_fusion.4
  122.8 1.2 fusion.108
  124.0 1.1 constant_dynamic-slice_fusion.4
  125.3 1.3 fusion.110
  126.6 2.7 fusion.111
  130.0 1.0 constant_dynamic-update-slice_fusion.2
  131.0 1.2 constant_dynamic-slice_fusion.5
  132.6 1.0 convolution_bitcast_fusion.2
  133.6 2.9 convolution_convert_fusion.4
  137.3 1.2 fusion.108
  138.5 1.1 constant_dynamic-slice_fusion.4
  139.8 1.3 fusion.110
  141.1 2.7 fusion.111
  144.4 1.0 constant_dynamic-update-slice_fusion.2
  145.5 1.2 constant_dynamic-slice_fusion.5
  148.1 2.9 convolution_convert_fusion.4
  151.8 1.2 fusion.108
  153.0 1.1 constant_dynamic-slice_fusion.4
  154.3 1.3 fusion.110
  155.6 2.7 fusion.111
  158.9 1.0 constant_dynamic-update-slice_fusion.2
  160.0 1.2 constant_dynamic-slice_fusion.5
  161.6 1.0 convolution_bitcast_fusion.2
  162.6 2.9 convolution_convert_fusion.4
  166.3 1.2 fusion.108
  167.5 1.1 constant_dynamic-slice_fusion.4
  168.8 1.3 fusion.110
  170.1 2.7 fusion.111
  173.4 1.0 constant_dynamic-update-slice_fusion.2
  174.5 10.4 %convert_bitcast_fusion = bf16[4,512,4096]{1,2,0:T(8,128)(2,1)} fusion(bf16[4,128,4096]{1,2,0:T(8,128)(2,1)} %get-tuple-element.163, bf16[4,128,512]{2,1,0:T(8,128)(2,1)S(1)} %get-tuple-element.165), kind=kOutput, calls=%fused_computation.43 | convolution fusion | flops 2155872256 | bytes 21495808 | tf_op jit(solution)/shard_map/eot,eov->etv/dot_general | solution.py:73
  185.0 6.4 %copy.35 = bf16[1,512,4096]{1,2,0:T(8,128)(2,1)} copy(bf16[1,512,4096]{2,1,0:T(8,128)(2,1)} %param.13) | data formatting | bytes 8388608 | tf_op args[5]
  191.4 119.8 %reduce-scatter.2.cloned.1.call-done = bf16[1,512,4096]{1,2,0:T(8,128)(2,1)} async-done(((bf16[4,512,4096]{1,2,0:T(8,128)(2,1)}), bf16[1,512,4096]{1,2,0:T(8,128)(2,1)}) %reduce-scatter.2.cloned.1.call-update) | async-done | bytes 4194320 | tf_op jit(solution)/shard_map/reduce_scatter | solution.py:72
  311.2 4.7 %add_convert_fusion = bf16[1,512,4096]{1,2,0:T(8,128)(2,1)S(1)} fusion(bf16[1,512,4096]{1,2,0:T(8,128)(2,1)} %reduce-scatter.2.cloned.1.call-done, bf16[1,512,4096]{1,2,0:T(8,128)(2,1)} %copy.35), kind=kLoop, calls=%fused_computation.45 | loop fusion | flops 10485760 | bytes 12582912 | tf_op jit(solution)/shard_map/convert_element_type | solution.py:80
  316.0 2.0 copy-done
  318.0 3.2 fusion.40
  321.1 6.3 %copy.38 = bf16[1,512,4096]{2,1,0:T(8,128)(2,1)} copy(bf16[1,512,4096]{1,2,0:T(8,128)(2,1)} %copy-done) | data formatting | bytes 8388608
  327.5 65.2 %all-reduce.2.cloned.1.call-done = bf16[512,512]{1,0:T(8,128)(2,1)} async-done(((bf16[512,512]{1,0:T(8,128)(2,1)}), bf16[512,512]{1,0:T(8,128)(2,1)}) %all-reduce.2.cloned.1.call-update) | async-done | bytes 524304 | tf_op jit(solution)/shard_map/psum | solution.py:82
  392.7 1.8 fusion.43
  395.2 2.1 fusion.46
  398.4 1.9 fusion.39
  401.3 1.9 fusion.47
  403.2 1.9 fusion.52
  405.0 1.9 fusion.38
  406.9 1.8 fusion.53
  408.8 9.2 %multiply_bitcast_fusion = f32[1,512,4096]{2,1,0:T(8,128)} fusion(f32[]{:T(128)S(6)} %add.29, f32[512,512]{1,0:T(8,128)S(1)} %fusion.53, bf16[1,512,4096]{1,2,0:T(8,128)(2,1)S(1)} %copy-done.1), kind=kOutput, calls=%fused_computation.44 | convolution fusion | flops 12889096192 | bytes 13631492 | tf_op jit(solution)/shard_map/dot_general | solution.py:97
  (58 shorter events, 12.9 us)
Async XLA Ops:
  7.2 109.3 %copy-start.2 = (bf16[4,128,512]{2,1,0:T(8,128)(2,1)S(1)}, bf16[4,128,512]{2,1,0:T(8,128)(2,1)}, u32[]{:S(2)}) copy-start(bf16[4,128,512]{2,1,0:T(8,128)(2,1)} %param.8) | copy-start | bytes 1572868
  7.2 109.3 %all-gather.2.cloned.1.call-start = ((), (), s32[]{:S(2)}) async-start(), calls=%async_computation.1 | async-start | bytes 20971520 | tf_op jit(solution)/shard_map/all_gather | solution.py:64
  7.9 303.3 %reduce-scatter.2.cloned.1.call-start = ((), (), s32[]{:S(2)}) async-start(), calls=%async_computation.2 | async-start | bytes 20971520 | tf_op jit(solution)/shard_map/reduce_scatter | solution.py:72
  129.9 1.1 copy-start.3
  144.4 1.1 copy-start.3
  158.9 1.1 copy-start.3
  173.4 1.1 copy-start.3
  184.9 207.7 %all-reduce.2.cloned.1.call-start = ((), (), s32[]{:S(2)}) async-start(), calls=%async_computation.3 | async-start | bytes 1048576 | tf_op jit(solution)/shard_map/psum | solution.py:82
  315.9 2.0 copy-start
  397.4 3.9 copy-start.4
  403.1 5.6 %copy-start.1 = (bf16[1,512,4096]{1,2,0:T(8,128)(2,1)S(1)}, bf16[1,512,4096]{1,2,0:T(8,128)(2,1)}, u32[]{:S(2)}) copy-start(bf16[1,512,4096]{1,2,0:T(8,128)(2,1)} %copy-done) | copy-start | bytes 12582916
Sparse Core Ops, SparseCore 0:
  9.6 106.8 all-gather.1
  185.1 126.1 reduce-scatter.1
  321.3 71.3 all-reduce.1
where the time goes:
time: 429 us; the launch traced here: 425 us
  waiting for transfers between devices  294 us (69%)
  matrix products  71.4 us (17%)
  local copies, waits for them, and re-layouts  32.3 us (8%)
  between operations  14.6 us (3%)
  other arithmetic  11.6 us (3%)
    reduce_scatter x1, waiting for transfers between devices, body(): lax.psum_scatter(jnp.einsum('eot,eov->etv', latent, key_value_gradient_to...  120 us
    all_gather x1, waiting for transfers between devices, body(): weights_all = lax.all_gather(key_value_up_weight, 'dp', axis=0, tiled=True)  109 us
    psum x1, waiting for transfers between devices, body(): lax.psum(jnp.dot(source, source.T, precision=highest).astype(jnp.bfloat16...  65.2 us
    unnamed x10, local copies, waits for them, and re-layouts  14.8 us
    dot_general x4, matrix products, layer_grads(): jnp.dot(compressed_latent_rows, weight_cols, preferred_element_type=jnp.f...  11.6 us
    dynamic_slice x16, local copies, waits for them, and re-layouts, body(): lax.scan(layer_body, 0, (latent, rope_keys, queries, grad_out, weights_all))  11.6 us
    dot_general x4, matrix products, layer_grads(): jnp.einsum('hst,shd->thd', grad_scores, query_nope, preferred_element_typ...  10.8 us
    dot_general x1, matrix products, body(): jnp.einsum('eot,eov->etv', latent, key_value_gradient_total, preferred_el...  10.4 us
  transfers between devices with their start and end apart: 3, of which 3 were waited for; matrix products, arithmetic and copies ran while one was open for 3% of the time, Pallas kernels for 0%

commit v1 on v0

v1 whole, which is shorter than its diff:
```python
import functools
import math

import jax
import jax.numpy as jnp
from jax import lax
from jax.experimental import pallas as pl
from jax.experimental.pallas import tpu as pltpu
from jax.sharding import PartitionSpec as P

NOPE = 128
ROPE = 64
VDIM = 128
STEPS = 2
PAIR = 2

poly_first = 3.4445
poly_second = -4.775
poly_third = 2.0315
norm_epsilon = 1e-07
decay_rate = 0.95

BF16 = jnp.bfloat16
F32 = jnp.float32
MESH = pl.DeviceIdType.MESH
NT = (((1,), (1,)), ((), ()))


def dot(a, b):
    return jnp.dot(a, b, preferred_element_type=F32)


def dot_nt(a, b):
    return lax.dot_general(a, b, NT, preferred_element_type=F32)


def split(a):
    high = a.astype(BF16)
    return high, (a - high.astype(F32)).astype(BF16)


def dot_wide(a, b):
    ah, al = split(a)
    bh, bl = split(b)
    return dot(ah, bh) + (dot(ah, bl) + dot(al, bh))


def greet(axis, n, me):
    barrier = pltpu.get_barrier_semaphore()
    for k in range(1, n):
        pl.semaphore_signal(
            barrier, inc=1, device_id={axis: lax.rem(me + k, n)}, device_id_type=MESH
        )
    pl.semaphore_wait(barrier, n - 1)


def grads_kernel(
    n, chunks, latent, rope, queries, grad_out, weight, momentum, fresh, gram,
    cbuf, rbuf, qbuf, obuf, wbuf, mbuf, fbuf, small_send, small_recv, big_send, big_recv,
    small_own, big_own, w_sem, m_sem, f_sem,
):
    me = lax.axis_index("dp")
    rows = latent.shape[1]
    width = latent.shape[2]
    qw = PAIR * (NOPE + ROPE)
    ow = PAIR * VDIM
    kw = PAIR * (NOPE + VDIM)
    score_scale = 1.0 / math.sqrt(NOPE + ROPE)

    def columns(c, w):
        return pl.ds(pl.multiple_of(c * w, 128), w)

    def small(k, i):
        to = lax.rem(me + k, n)
        src, dst = ((latent, cbuf), (rope, rbuf))[i]
        return pltpu.make_async_remote_copy(
            src_ref=src.at[to], dst_ref=dst.at[me], send_sem=small_send.at[k - 1, i],
            recv_sem=small_recv.at[k - 1, i], device_id={"dp": to}, device_id_type=MESH,
        )

    def big(k, c, i):
        to = lax.rem(me + k, n)
        src, dst, w = ((queries, qbuf, qw), (grad_out, obuf, ow))[i]
        return pltpu.make_async_remote_copy(
            src_ref=src.at[to, :, columns(c, w)], dst_ref=dst.at[me, :, columns(c, w)],
            send_sem=big_send.at[k - 1, c, i], recv_sem=big_recv.at[k - 1, c, i],
            device_id={"dp": to}, device_id_type=MESH,
        )

    def small_mine(i):
        src, dst = ((latent, cbuf), (rope, rbuf))[i]
        return pltpu.make_async_copy(src.at[me], dst.at[me], small_own.at[i])

    def big_mine(c, i):
        src, dst, w = ((queries, qbuf, qw), (grad_out, obuf, ow))[i]
        return pltpu.make_async_copy(
            src.at[me, :, columns(c, w)], dst.at[me, :, columns(c, w)], big_own.at[c, i]
        )

    def w_copy(c):
        return pltpu.make_async_copy(
            weight.at[:, columns(c, kw)], wbuf.at[:, columns(c, kw)], w_sem.at[c]
        )

    def m_copy(c):
        return pltpu.make_async_copy(
            momentum.at[:, columns(c, kw)], mbuf.at[:, columns(c, kw)], m_sem.at[c]
        )

    def f_copy(c):
        return pltpu.make_async_copy(
            fbuf.at[:, columns(c, kw)], fresh.at[:, columns(c, kw)], f_sem.at[c]
        )

    greet("dp", n, me)
    for i in range(2):
        for k in range(1, n):
            small(k, i).start()
        small_mine(i).start()

    def begin(c, carry):
        for i in range(2):
            for k in range(1, n):
                big(k, c, i).start()
            big_mine(c, i).start()
        w_copy(c).start()
        m_copy(c).start()
        return carry

    lax.fori_loop(0, chunks, begin, 0)
    gram[...] = jnp.zeros_like(gram)
    for i in range(2):
        for k in range(1, n):
            small(k, i).wait_recv()
        small_mine(i).wait()

    earlier = lax.broadcasted_iota(jnp.int32, (rows, rows), 0)
    later = lax.broadcasted_iota(jnp.int32, (rows, rows), 1)
    allowed = earlier <= later

    def work(c, carry):
        for i in range(2):
            for k in range(1, n):
                big(k, c, i).wait_recv()
            big_mine(c, i).wait()
        w_copy(c).wait()
        m_copy(c).wait()
        latents = cbuf[...].reshape(n * rows, width)
        kv = dot(latents, wbuf[:, columns(c, kw)]).astype(BF16)
        parts = []
        for g in range(n):
            here = kv[g * rows:(g + 1) * rows]
            q_all = qbuf[g, :, columns(c, qw)]
            o_all = obuf[g, :, columns(c, ow)]
            for h in range(PAIR):
                key = here[:, h * 256:h * 256 + NOPE]
                value = here[:, h * 256 + NOPE:(h + 1) * 256]
                q_nope = q_all[:, h * 192:h * 192 + NOPE]
                q_rope = q_all[:, h * 192 + NOPE:(h + 1) * 192]
                out_grad = o_all[:, h * VDIM:(h + 1) * VDIM]
                scores = (dot_nt(key, q_nope) + dot_nt(rbuf[g], q_rope)) * score_scale
                scores = jnp.where(allowed, scores, -jnp.inf)
                expd = jnp.exp(scores - jnp.max(scores, axis=0, keepdims=True))
                probs = expd * (1.0 / jnp.sum(expd, axis=0, keepdims=True))
                grad_value = dot(probs.astype(BF16), out_grad)
                grad_probs = dot_nt(value, out_grad)
                delta = jnp.sum(probs * grad_probs, axis=0, keepdims=True)
                grad_scores = (probs * (grad_probs - delta) * score_scale).astype(BF16)
                parts.append(dot(grad_scores, q_nope).astype(BF16))
                parts.append(grad_value.astype(BF16))
        joined = jnp.concatenate(
            [
                jnp.concatenate(parts[g * 2 * PAIR:(g + 1) * 2 * PAIR], axis=1)
                for g in range(n)
            ],
            axis=0,
        )
        grad = lax.dot_general(
            latents, joined, (((0,), (0,)), ((), ())), preferred_element_type=F32
        )
        new = (decay_rate * mbuf[:, columns(c, kw)].astype(F32) + grad).astype(BF16)
        fbuf[:, columns(c, kw)] = new
        gram[...] += dot_nt(new, new)
        f_copy(c).start()
        return carry

    lax.fori_loop(0, chunks, work, 0)

    for i in range(2):
        for k in range(1, n):
            small(k, i).wait_send()

    def finish(c, carry):
        for i in range(2):
            for k in range(1, n):
                big(k, c, i).wait_send()
        f_copy(c).wait()
        return carry

    lax.fori_loop(0, chunks, finish, 0)


def mixer_kernel(
    n, update_scale, gram, high, low, mine, sums, total, first_send, first_recv,
    second_send, second_recv,
):
    me = lax.axis_index("heads")
    size = gram.shape[0]
    block = size // n
    mine[...] = gram[...].astype(BF16).reshape(n, block, size)

    def first(k):
        to = lax.rem(me + k, n)
        return pltpu.make_async_remote_copy(
            src_ref=mine.at[to], dst_ref=sums.at[k - 1], send_sem=first_send.at[k - 1],
            recv_sem=first_recv.at[k - 1], device_id={"heads": to}, device_id_type=MESH,
        )

    def second(k):
        to = lax.rem(me + k, n)
        return pltpu.make_async_remote_copy(
            src_ref=total.at[me], dst_ref=total.at[me], send_sem=second_send.at[k - 1],
            recv_sem=second_recv.at[k - 1], device_id={"heads": to}, device_id_type=MESH,
        )

    greet("heads", n, me)
    for k in range(1, n):
        first(k).start()
    added = mine[me].astype(F32)
    for k in range(1, n):
        first(k).wait_recv()
        added = added + sums[k - 1].astype(F32)
    total[me] = added.astype(BF16)
    for k in range(1, n):
        second(k).start()
    for k in range(1, n):
        second(k).wait_recv()

    raw = total[...].reshape(size, size).astype(F32)
    row = lax.broadcasted_iota(jnp.int32, (size, size), 0)
    col = lax.broadcasted_iota(jnp.int32, (size, size), 1)
    diagonal = row == col
    trace = jnp.sum(
        jnp.sum(jnp.where(diagonal, raw, 0.0), axis=0, keepdims=True), axis=1, keepdims=True
    )
    norm = jnp.sqrt(trace) + norm_epsilon
    base = raw / (norm * norm)
    identity = jnp.where(diagonal, 1.0, 0.0)
    mixer = None
    for step in range(STEPS):
        inner = base if mixer is None else dot_wide(dot_wide(mixer, base), mixer)
        poly = poly_first * identity + poly_second * inner + poly_third * dot_wide(inner, inner)
        mixer = poly if mixer is None else dot_wide(poly, mixer)
    top, rest = split(mixer * (update_scale / norm))
    high[...] = top
    low[...] = rest
    for k in range(1, n):
        first(k).wait_send()
        second(k).wait_send()


def update_kernel(high, low, fresh, kept, update):
    new = fresh[...]
    kept[0] = new
    update[0] = dot(high[...], new) + dot(low[...], new)


def body(n_dp, n_heads, update_scale, latent, rope, queries, grad_out, weight, momentum):
    rows, width = latent.shape[1:]
    heads_here = grad_out.shape[2] // VDIM
    chunks = heads_here // PAIR
    cols = weight.shape[2]
    hbm = pl.BlockSpec(memory_space=pl.ANY)
    vmem = pl.BlockSpec(memory_space=pltpu.VMEM)
    dma = pltpu.SemaphoreType.DMA
    fresh, gram = pl.pallas_call(
        functools.partial(grads_kernel, n_dp, chunks),
        out_shape=(
            jax.ShapeDtypeStruct((width, cols), BF16),
            jax.ShapeDtypeStruct((width, width), F32),
        ),
        in_specs=[hbm] * 6,
        out_specs=(hbm, vmem),
        scratch_shapes=[
            pltpu.VMEM((n_dp, rows, width), BF16),
            pltpu.VMEM((n_dp, rows, ROPE), BF16),
            pltpu.VMEM((n_dp, rows, queries.shape[2]), BF16),
            pltpu.VMEM((n_dp, rows, grad_out.shape[2]), BF16),
            pltpu.VMEM((width, cols), BF16),
            pltpu.VMEM((width, cols), BF16),
            pltpu.VMEM((width, cols), BF16),
            dma((n_dp - 1, 2)),
            dma((n_dp - 1, 2)),
            dma((n_dp - 1, chunks, 2)),
            dma((n_dp - 1, chunks, 2)),
            dma((2,)),
            dma((chunks, 2)),
            dma((chunks,)),
            dma((chunks,)),
            dma((chunks,)),
        ],
        compiler_params=pltpu.CompilerParams(
            collective_id=0, has_side_effects=True, vmem_limit_bytes=48 * 2**20
        ),
        name="grads",
    )(latent, rope, queries, grad_out, weight[0], momentum[0])

    block = width // n_heads
    high, low = pl.pallas_call(
        functools.partial(mixer_kernel, n_heads, update_scale),
        out_shape=(jax.ShapeDtypeStruct((width, width), BF16),) * 2,
        in_specs=[vmem],
        out_specs=(vmem, vmem),
        scratch_shapes=[
            pltpu.VMEM((n_heads, block, width), BF16),
            pltpu.VMEM((n_heads - 1, block, width), BF16),
            pltpu.VMEM((n_heads, block, width), BF16),
            dma((n_heads - 1,)),
            dma((n_heads - 1,)),
            dma((n_heads - 1,)),
            dma((n_heads - 1,)),
        ],
        compiler_params=pltpu.CompilerParams(
            collective_id=1, has_side_effects=True, vmem_limit_bytes=48 * 2**20
        ),
        name="mixer",
    )(gram)

    tile = 512
    return pl.pallas_call(
        update_kernel,
        grid=(cols // tile,),
        out_shape=(
            jax.ShapeDtypeStruct((1, width, cols), BF16),
            jax.ShapeDtypeStruct((1, width, cols), F32),
        ),
        in_specs=[
            pl.BlockSpec((width, width), lambda j: (0, 0)),
            pl.BlockSpec((width, width), lambda j: (0, 0)),
            pl.BlockSpec((width, tile), lambda j: (0, j)),
        ],
        out_specs=(
            pl.BlockSpec((1, width, tile), lambda j: (0, 0, j)),
            pl.BlockSpec((1, width, tile), lambda j: (0, 0, j)),
        ),
        compiler_params=pltpu.CompilerParams(vmem_limit_bytes=32 * 2**20),
        name="update",
    )(high, low, fresh)


def solution(mesh):
    n_dp = mesh.shape["dp"]
    n_heads = mesh.shape["heads"]
    placed = (
        P(None, "dp", None),
        P(None, "dp", None),
        P(None, "dp", "heads"),
        P(None, "dp", "heads"),
        P("dp", None, "heads"),
        P("dp", None, "heads"),
    )

    def whole(latent, rope_keys, queries, grad_out, key_value_up_weight, momentum):
        _, width, cols = key_value_up_weight.shape
        update_scale = 0.2 * math.sqrt(max(width, cols))
        return jax.shard_map(
            functools.partial(body, n_dp, n_heads, update_scale),
            mesh=mesh,
            in_specs=placed,
            out_specs=(P("dp", None, "heads"), P("dp", None, "heads")),
            check_vma=False,
        )(latent, rope_keys, queries, grad_out, key_value_up_weight, momentum)

    return whole
```

time: 429 us -> 119 us (0.28)
  waiting for transfers between devices: 294 us -> 0 us
  Pallas kernels: 0 us -> 112 us
  matrix products: 71.4 us -> 0 us
  local copies, waits for them, and re-layouts: 32.3 us -> 5.77 us
  between operations: 14.6 us -> 0.67 us
  other arithmetic: 11.6 us -> 0 us
    reduce_scatter x1 -> x0, waiting for transfers between devices: 120 us -> none  [body(): lax.psum_scatter(jnp.einsum('eot,eov->etv', latent, key_value_gradient_to...]
    pallas_call x0 -> x3, Pallas kernels: none -> 112 us  [the longest x1 70.2 us: body(): pl.pallas_call(functools.partial(grads_kernel, n_dp, chunks), out_shape=(...]
    all_gather x1 -> x0, waiting for transfers between devices: 109 us -> none  [body(): weights_all = lax.all_gather(key_value_up_weight, 'dp', axis=0, tiled=True)]
    dot_general x35 -> x0, matrix products: 71.4 us -> none  [the longest x4 11.6 us: layer_grads(): jnp.dot(compressed_latent_rows, weight_cols, preferred_element_type=jnp.f...]
    psum x1 -> x0, waiting for transfers between devices: 65.2 us -> none  [body(): lax.psum(jnp.dot(source, source.T, precision=highest).astype(jnp.bfloat16...]
    dynamic_slice x16 -> x0, local copies, waits for them, and re-layouts: 11.6 us -> none  [body(): lax.scan(layer_body, 0, (latent, rope_keys, queries, grad_out, weights_all))]
    unnamed x10 -> x7, local copies, waits for them, and re-layouts: 14.8 us -> 5.77 us
    convert_element_type x1 -> x0, other arithmetic: 4.72 us -> none  [body(): (decay_rate * momentum.astype(jnp.float32) + grads).astype(jnp.bfloat16)]
  transfers between devices with their start and end apart: 3 -> 0, of which waited for: 3 -> 0; matrix products, arithmetic and copies ran while one was open for 3% -> 0% of each run, Pallas kernels for 0% -> 0%
where the time goes in v1:
time: 119 us
  Pallas kernels  112 us (94%)
  local copies, waits for them, and re-layouts  5.77 us (5%)
    pallas_call x1, Pallas kernels, body(): pl.pallas_call(functools.partial(grads_kernel, n_dp, chunks), out_shape=(...  70.2 us
    pallas_call x1, Pallas kernels, body(): pl.pallas_call(functools.partial(mixer_kernel, n_heads, update_scale), ou...  34.5 us
    pallas_call x1, Pallas kernels, body(): pl.pallas_call(update_kernel, grid=(cols // tile,), out_shape=(jax.ShapeD...  7.67 us
    unnamed x7, local copies, waits for them, and re-layouts  5.77 us

profile of v1, /device:TPU:24, one launch (start us, length us, event | category | flops | bytes accessed | tf_op | source)
XLA Modules:
  0.0 118.8 jit_solution(9722109498258106241)
XLA Ops:
  0.6 1.0 copy.8.rope
  1.6 0.0 copy-start.1
  1.6 1.6 %copy-done.1 = bf16[4,128,2048]{2,1,0:T(8,128)(2,1)S(1)} copy-done((bf16[4,128,2048]{2,1,0:T(8,128)(2,1)S(1)}, bf16[4,128,2048]{2,1,0:T(8,128)(2,1)}, u32[]{:S(2)}) %copy-start.1) | copy-done | bytes 2097176
  3.2 0.0 copy-start.2
  3.2 1.0 copy-done.2
  4.2 70.2 %grads.1 = (bf16[512,4096]{1,0:T(8,128)(2,1)}, f32[512,512]{1,0:T(8,128)S(1)}) custom-call(bf16[4,128,512]{2,1,0:T(8,128)(2,1)S(1)} %copy-done.2, bf16[4,128,64]{2,1,0:T(8,128)(2,1)S(1)} %copy.8.rope, bf16[4,128,3072]{2,1,0:T(8,128)(2,1)} %queries.1, bf16[4,128,2048]{2,1,0:T(8,128)(2,1)S(1)} %copy-done.1, bf16[512,4096]{1,0:T(8,128)(2,1)} %bitcast.2, ...), custom_call_target="tpu_custom_call" | custom-call | tf_op jit(solution)/shard_map/grads/pallas_call | solution.py:276
  74.4 34.5 %mixer.1 = (bf16[512,512]{1,0:T(8,128)(2,1)S(1)}, bf16[512,512]{1,0:T(8,128)(2,1)S(1)}) custom-call(f32[512,512]{1,0:T(8,128)S(1)} %get-tuple-element.6.gram), custom_call_target="tpu_custom_call" | custom-call | tf_op jit(solution)/shard_map/mixer/pallas_call | solution.py:309
  108.9 0.0 copy-start
  108.9 2.2 %copy-done = bf16[512,4096]{1,0:T(8,128)(2,1)S(1)} copy-done((bf16[512,4096]{1,0:T(8,128)(2,1)S(1)}, bf16[512,4096]{1,0:T(8,128)(2,1)}, u32[]{:S(2)}) %copy-start) | copy-done | bytes 4194328
  111.1 7.7 %update.1 = (bf16[1,512,4096]{2,1,0:T(8,128)(2,1)}, f32[1,512,4096]{2,1,0:T(8,128)}) custom-call(bf16[512,512]{1,0:T(8,128)(2,1)S(1)} %get-tuple-element.7.high, bf16[512,512]{1,0:T(8,128)(2,1)S(1)} %get-tuple-element.8.low, bf16[512,4096]{1,0:T(8,128)(2,1)S(1)} %copy-done), custom_call_target="tpu_custom_call" | custom-call | tf_op jit(solution)/shard_map/update/pallas_call | solution.py:330
Async XLA Ops:
  1.6 1.6 %copy-start.1 = (bf16[4,128,2048]{2,1,0:T(8,128)(2,1)S(1)}, bf16[4,128,2048]{2,1,0:T(8,128)(2,1)}, u32[]{:S(2)}) copy-start(bf16[4,128,2048]{2,1,0:T(8,128)(2,1)} %grad_out.1) | copy-start | bytes 6291460
  3.2 1.0 copy-start.2
  108.9 2.2 %copy-start = (bf16[512,4096]{1,0:T(8,128)(2,1)S(1)}, bf16[512,4096]{1,0:T(8,128)(2,1)}, u32[]{:S(2)}) copy-start(bf16[512,4096]{1,0:T(8,128)(2,1)} %get-tuple-element.9.fresh) | copy-start | bytes 12582916

commit v2 on v1

--- a/solution.py
+++ b/solution.py
@@ -13,6 +13,7 @@
 VDIM = 128
 STEPS = 2
 PAIR = 2
+TILE = 128
 
 poly_first = 3.4445
 poly_second = -4.775
@@ -45,6 +46,11 @@
     return dot(ah, bh) + (dot(ah, bl) + dot(al, bh))
 
 
+def upper(size):
+    blocks = size // TILE
+    return [(i, j) for i in range(blocks) for j in range(i, blocks)]
+
+
 def greet(axis, n, me):
     barrier = pltpu.get_barrier_semaphore()
     for k in range(1, n):
@@ -55,8 +61,8 @@
 
 
 def grads_kernel(
-    n, chunks, latent, rope, queries, grad_out, weight, momentum, fresh, gram,
-    cbuf, rbuf, qbuf, obuf, wbuf, mbuf, fbuf, small_send, small_recv, big_send, big_recv,
+    n, chunks, latent, rope, queries, grad_out, weight, momentum, fresh, packed,
+    cbuf, rbuf, turned, qbuf, obuf, wbuf, mbuf, fbuf, whole, small_send, small_recv, big_send, big_recv,
     small_own, big_own, w_sem, m_sem, f_sem,
 ):
     me = lax.axis_index("dp")
@@ -128,11 +134,14 @@
         return carry
 
     lax.fori_loop(0, chunks, begin, 0)
-    gram[...] = jnp.zeros_like(gram)
+    whole[...] = jnp.zeros_like(whole)
     for i in range(2):
         for k in range(1, n):
             small(k, i).wait_recv()
         small_mine(i).wait()
+
+    for g in range(n):
+        turned[g] = rbuf[g].astype(F32).T.astype(BF16)
 
     earlier = lax.broadcasted_iota(jnp.int32, (rows, rows), 0)
     later = lax.broadcasted_iota(jnp.int32, (rows, rows), 1)
@@ -158,7 +167,7 @@
                 q_nope = q_all[:, h * 192:h * 192 + NOPE]
                 q_rope = q_all[:, h * 192 + NOPE:(h + 1) * 192]
                 out_grad = o_all[:, h * VDIM:(h + 1) * VDIM]
-                scores = (dot_nt(key, q_nope) + dot_nt(rbuf[g], q_rope)) * score_scale
+                scores = (dot_nt(key, q_nope) + dot_nt(turned[g], q_rope)) * score_scale
                 scores = jnp.where(allowed, scores, -jnp.inf)
                 expd = jnp.exp(scores - jnp.max(scores, axis=0, keepdims=True))
                 probs = expd * (1.0 / jnp.sum(expd, axis=0, keepdims=True))
@@ -180,11 +189,15 @@
         )
         new = (decay_rate * mbuf[:, columns(c, kw)].astype(F32) + grad).astype(BF16)
         fbuf[:, columns(c, kw)] = new
-        gram[...] += dot_nt(new, new)
+        whole[...] += dot_nt(new, new)
         f_copy(c).start()
         return carry
 
     lax.fori_loop(0, chunks, work, 0)
+    for p, (i, j) in enumerate(upper(width)):
+        packed[pl.ds(p * TILE, TILE), :] = whole[
+            pl.ds(i * TILE, TILE), pl.ds(j * TILE, TILE)
+        ].astype(BF16)
 
     for i in range(2):
         for k in range(1, n):
@@ -201,42 +214,50 @@
 
 
 def mixer_kernel(
-    n, update_scale, gram, high, low, mine, sums, total, first_send, first_recv,
+    n, update_scale, mine, high, low, sums, total, full, first_send, first_recv,
     second_send, second_recv,
 ):
     me = lax.axis_index("heads")
-    size = gram.shape[0]
-    block = size // n
-    mine[...] = gram[...].astype(BF16).reshape(n, block, size)
+    size = high.shape[0]
+    pairs = upper(size)
+    block = len(pairs) * TILE // n
+
+    def part(k):
+        return pl.ds(pl.multiple_of(k * block, 16), block)
 
     def first(k):
         to = lax.rem(me + k, n)
         return pltpu.make_async_remote_copy(
-            src_ref=mine.at[to], dst_ref=sums.at[k - 1], send_sem=first_send.at[k - 1],
+            src_ref=mine.at[part(to)], dst_ref=sums.at[k - 1], send_sem=first_send.at[k - 1],
             recv_sem=first_recv.at[k - 1], device_id={"heads": to}, device_id_type=MESH,
         )
 
     def second(k):
         to = lax.rem(me + k, n)
         return pltpu.make_async_remote_copy(
-            src_ref=total.at[me], dst_ref=total.at[me], send_sem=second_send.at[k - 1],
+            src_ref=total.at[part(me)], dst_ref=total.at[part(me)], send_sem=second_send.at[k - 1],
             recv_sem=second_recv.at[k - 1], device_id={"heads": to}, device_id_type=MESH,
         )
 
     greet("heads", n, me)
     for k in range(1, n):
         first(k).start()
-    added = mine[me].astype(F32)
+    added = mine[part(me), :].astype(F32)
     for k in range(1, n):
         first(k).wait_recv()
         added = added + sums[k - 1].astype(F32)
-    total[me] = added.astype(BF16)
+    total[part(me), :] = added.astype(BF16)
     for k in range(1, n):
         second(k).start()
     for k in range(1, n):
         second(k).wait_recv()
 
-    raw = total[...].reshape(size, size).astype(F32)
+    for p, (i, j) in enumerate(pairs):
+        here = total[pl.ds(p * TILE, TILE), :].astype(F32)
+        full[pl.ds(i * TILE, TILE), pl.ds(j * TILE, TILE)] = here
+        if i != j:
+            full[pl.ds(j * TILE, TILE), pl.ds(i * TILE, TILE)] = here.T
+    raw = full[...]
     row = lax.broadcasted_iota(jnp.int32, (size, size), 0)
     col = lax.broadcasted_iota(jnp.int32, (size, size), 1)
     diagonal = row == col
@@ -269,26 +290,29 @@
     rows, width = latent.shape[1:]
     heads_here = grad_out.shape[2] // VDIM
     chunks = heads_here // PAIR
+    packed = len(upper(width)) * TILE
     cols = weight.shape[2]
-    hbm = pl.BlockSpec(memory_space=pl.ANY)
+    hbm = pl.BlockSpec(memory_space=pltpu.HBM)
     vmem = pl.BlockSpec(memory_space=pltpu.VMEM)
     dma = pltpu.SemaphoreType.DMA
     fresh, gram = pl.pallas_call(
         functools.partial(grads_kernel, n_dp, chunks),
         out_shape=(
             jax.ShapeDtypeStruct((width, cols), BF16),
-            jax.ShapeDtypeStruct((width, width), F32),
+            jax.ShapeDtypeStruct((packed, TILE), BF16),
         ),
         in_specs=[hbm] * 6,
         out_specs=(hbm, vmem),
         scratch_shapes=[
             pltpu.VMEM((n_dp, rows, width), BF16),
+            pltpu.VMEM((n_dp, ROPE, rows), BF16),
             pltpu.VMEM((n_dp, rows, ROPE), BF16),
             pltpu.VMEM((n_dp, rows, queries.shape[2]), BF16),
             pltpu.VMEM((n_dp, rows, grad_out.shape[2]), BF16),
             pltpu.VMEM((width, cols), BF16),
             pltpu.VMEM((width, cols), BF16),
             pltpu.VMEM((width, cols), BF16),
+            pltpu.VMEM((width, width), F32),
             dma((n_dp - 1, 2)),
             dma((n_dp - 1, 2)),
             dma((n_dp - 1, chunks, 2)),
@@ -300,28 +324,28 @@
             dma((chunks,)),
         ],
         compiler_params=pltpu.CompilerParams(
-            collective_id=0, has_side_effects=True, vmem_limit_bytes=48 * 2**20
+            collective_id=0, has_side_effects=True, vmem_limit_bytes=56 * 2**20
         ),
         name="grads",
-    )(latent, rope, queries, grad_out, weight[0], momentum[0])
-
-    block = width // n_heads
+    )(latent, jnp.swapaxes(rope, 1, 2), queries, grad_out, weight[0], momentum[0])
+
+    block = packed // n_heads
     high, low = pl.pallas_call(
         functools.partial(mixer_kernel, n_heads, update_scale),
         out_shape=(jax.ShapeDtypeStruct((width, width), BF16),) * 2,
         in_specs=[vmem],
         out_specs=(vmem, vmem),
         scratch_shapes=[
-            pltpu.VMEM((n_heads, block, width), BF16),
-            pltpu.VMEM((n_heads - 1, block, width), BF16),
-            pltpu.VMEM((n_heads, block, width), BF16),
+            pltpu.VMEM((n_heads - 1, block, TILE), BF16),
+            pltpu.VMEM((packed, TILE), BF16),
+            pltpu.VMEM((width, width), F32),
             dma((n_heads - 1,)),
             dma((n_heads - 1,)),
             dma((n_heads - 1,)),
             dma((n_heads - 1,)),
         ],
         compiler_params=pltpu.CompilerParams(
-            collective_id=1, has_side_effects=True, vmem_limit_bytes=48 * 2**20
+            collective_id=1, has_side_effects=True, vmem_limit_bytes=24 * 2**20
         ),
         name="mixer",
     )(gram)
@@ -343,7 +367,7 @@
             pl.BlockSpec((1, width, tile), lambda j: (0, 0, j)),
             pl.BlockSpec((1, width, tile), lambda j: (0, 0, j)),
         ),
-        compiler_params=pltpu.CompilerParams(vmem_limit_bytes=32 * 2**20),
+        compiler_params=pltpu.CompilerParams(vmem_limit_bytes=52 * 2**20),
         name="update",
     )(high, low, fresh)
 

time: 119 us -> 109 us (0.916)
  Pallas kernels: 112 us -> 107 us
  local copies, waits for them, and re-layouts: 5.77 us -> 0.97 us
    pallas_call x1, Pallas kernels: 34.5 us -> 26.2 us  [body(): pl.pallas_call(functools.partial(mixer_kernel, n_heads, update_scale), ou...]
    unnamed x7 -> x2, local copies, waits for them, and re-layouts: 5.77 us -> 0.97 us
    pallas_call x1, Pallas kernels: 7.67 us -> 9.95 us  [body(): pl.pallas_call(update_kernel, grid=(cols // tile,), out_shape=(jax.ShapeD...]
where the time goes in v2:
time: 109 us; the launch traced here: 108 us
  Pallas kernels  107 us (98%)
    pallas_call x1, Pallas kernels, body(): pl.pallas_call(functools.partial(grads_kernel, n_dp, chunks), out_shape=(...  70.5 us
    pallas_call x1, Pallas kernels, body(): pl.pallas_call(functools.partial(mixer_kernel, n_heads, update_scale), ou...  26.2 us
    pallas_call x1, Pallas kernels, body(): pl.pallas_call(update_kernel, grid=(cols // tile,), out_shape=(jax.ShapeD...  9.95 us

profile of v2, /device:TPU:24, one launch (start us, length us, event | category | flops | bytes accessed | tf_op | source)
XLA Modules:
  0.0 108.2 jit_solution(3660933049322132690)
XLA Ops:
  0.6 70.5 %grads.1 = (bf16[512,4096]{1,0:T(8,128)(2,1)}, bf16[1280,128]{1,0:T(8,128)(2,1)}) custom-call(bf16[4,128,512]{2,1,0:T(8,128)(2,1)} %latent.1, bf16[4,64,128]{2,1,0:T(8,128)(2,1)} %bitcast.5, bf16[4,128,3072]{2,1,0:T(8,128)(2,1)} %queries.1, bf16[4,128,2048]{2,1,0:T(8,128)(2,1)} %grad_out.1, bf16[512,4096]{1,0:T(8,128)(2,1)} %bitcast.3, bf16[512,4096]{1,0:T(8,128)(2,1)} %bitcast.4), custom_call_target="tpu_custom_call" | custom-call | tf_op jit(solution)/shard_map/grads/pallas_call | solution.py:298
  71.1 0.0 copy-start
  71.1 1.0 copy-done
  72.1 26.2 %mixer.1 = (bf16[512,512]{1,0:T(8,128)(2,1)S(1)}, bf16[512,512]{1,0:T(8,128)(2,1)S(1)}) custom-call(bf16[1280,128]{1,0:T(8,128)(2,1)S(1)} %copy-done), custom_call_target="tpu_custom_call" | custom-call | tf_op jit(solution)/shard_map/mixer/pallas_call | solution.py:333
  98.2 9.9 %update.1 = (bf16[1,512,4096]{2,1,0:T(8,128)(2,1)}, f32[1,512,4096]{2,1,0:T(8,128)}) custom-call(bf16[512,512]{1,0:T(8,128)(2,1)S(1)} %get-tuple-element.7.high, bf16[512,512]{1,0:T(8,128)(2,1)S(1)} %get-tuple-element.8.low, bf16[512,4096]{1,0:T(8,128)(2,1)} %get-tuple-element.9.fresh), custom_call_target="tpu_custom_call" | custom-call | tf_op jit(solution)/shard_map/update/pallas_call | solution.py:354
Async XLA Ops:
  71.1 1.0 copy-start
